TPU v7x, 256 devices: a whole 4x4x8 slice. The times are simulated.
256 devices in a mesh: dp: 8 (over x, core), clus: 32 (over z, y).
Axes of the slice: x: 4, y: 4, z: 8, core: 2. Of those that a mesh axis runs over, the one named last changes fastest.
Arguments:
- activations: bfloat16 [1024, 12288], P('clus', 'dp'), may hold values from -6 to 6
- picks: int32 [1024, 48], replicated, may hold values from 0 to 383, all different within a row
- up_weight: bfloat16 [384, 12288, 128], P('clus', 'dp'), may hold values from -0.0546875 to 0.0546875
- up_bias: float32 [384, 128], P('clus'), may hold values from -3 to 3
- down_weight: bfloat16 [384, 128, 12288], P('clus', None, 'dp'), may hold values from -0.078125 to 0.078125
Outputs:
- layer_out: bfloat16 [1024, 12288], P('clus', 'dp')
Inputs may be any that keep to these rules, and one draw needn't show every extreme that they name: `picks`: each row names 48 distinct clusters; every cluster is named by some row.
All inputs are finite; a program needn't handle non-finite values.
Results may differ from a plain program's by a relative error of at most 0.012.
Values may be sent and summed in bfloat16 or wider, within the bound.
No kernel may reach another device: no remote copies, remote signals or barrier semaphores. Data moves between devices by JAX's collectives and lax.ppermute only.
A program may use at most 64 MiB of HBM per device.

v0:
```python
import jax
import jax.numpy as jnp
from jax import lax
from jax.sharding import PartitionSpec as P


def on_device(activations, picks, up_weight, up_bias, down_weight):
    tok_rows = activations.shape[0]
    clusters_here = up_weight.shape[0]
    ngroups = lax.axis_size("clus")
    own_index = lax.axis_index("clus")
    wanted = own_index * clusters_here + jnp.arange(clusters_here, dtype=jnp.int32)
    cluster_mask = jnp.any(picks[:, :, None] == wanted[None, None, :], axis=1).astype(jnp.float32)
    partial_pre = jnp.einsum(
        "rd,cdn->rcn",
        lax.all_gather(activations, "clus", axis=0, tiled=True),
        up_weight,
        preferred_element_type=jnp.float32,
    )
    summed = lax.psum(partial_pre, "dp")
    hidden = (jnp.maximum(summed + up_bias[None], 0.0) * cluster_mask[:, :, None]).astype(
        jnp.bfloat16
    )
    produced = jnp.einsum(
        "rcn,cnd->rd", hidden, down_weight, preferred_element_type=jnp.float32
    ).astype(jnp.bfloat16)
    returned = lax.all_to_all(produced, "clus", split_axis=0, concat_axis=0, tiled=True)
    combined = jnp.sum(returned.reshape(ngroups, tok_rows, -1).astype(jnp.float32), axis=0)
    return combined.astype(jnp.bfloat16)


def solution(mesh):
    placed = (P("clus", "dp"), P(), P("clus", "dp", None), P("clus", None), P("clus", None, "dp"))
    return jax.shard_map(
        on_device, mesh=mesh, in_specs=placed, out_specs=P("clus", "dp"), check_vma=False
    )
```

profile of v0, /device:TPU:19, one launch (start us, length us, event | category | flops | bytes accessed | tf_op | source)
XLA Modules:
  0.0 287.9 jit_solution(2460039226780015000)
XLA Ops:
  6.5 0.0 all-gather.2.cloned.1.call-start
  6.5 0.7 all-gather.2.cloned.1.call-update
  7.3 0.0 all-reduce.2.cloned.1.call-start
  7.3 80.6 %all-gather.2.cloned.1.call-done = bf16[1024,1536]{1,0:T(8,128)(2,1)} async-done(((bf16[32,1536]{1,0:T(8,128)(2,1)}), bf16[1024,1536]{1,0:T(8,128)(2,1)}) %all-gather.2.cloned.1.call-update) | async-done | bytes 3145744 | tf_op jit(solution)/shard_map/all_gather | solution.py:16
  87.9 9.7 %fusion = f32[1024,12,128]{2,0,1:T(8,128)} fusion(bf16[12,1536,128]{2,1,0:T(8,128)(2,1)} %param.7, bf16[1024,1536]{1,0:T(8,128)(2,1)} %all-gather.2.cloned.1.call-done), kind=kOutput, calls=%fused_computation.2 | convolution fusion | flops 4831838208 | bytes 14155776 | tf_op jit(solution)/shard_map/rd,cdn->rcn/dot_general | solution.py:14
  97.6 0.0 copy-start
  97.6 0.0 copy-start.1
  97.6 0.0 all-reduce.2.cloned.1.call-update
  97.7 0.9 copy-done
  98.5 0.4 compare_reduce_fusion
  99.0 88.9 %all-reduce.2.cloned.1.call-done = f32[1024,12,128]{2,0,1:T(8,128)} async-done(((f32[1024,12,128]{2,0,1:T(8,128)}), f32[1024,12,128]{2,0,1:T(8,128)}) %all-reduce.2.cloned.1.call-update) | async-done | bytes 6291472 | tf_op jit(solution)/shard_map/psum | solution.py:20
  187.9 0.0 copy-done.1
  187.9 8.6 %bitcast_convert_fusion = bf16[1024,1536]{1,0:T(8,128)(2,1)S(1)} fusion(bf16[12,128,1536]{2,1,0:T(8,128)(2,1)} %param.9, f32[1024,12,128]{2,0,1:T(8,128)} %all-reduce.2.cloned.1.call-done, f32[1024,12]{0,1:T(8,128)S(1)} %convert_element_type.15, f32[12,128]{1,0:T(8,128)S(1)} %copy-done.1), kind=kOutput, calls=%fused_computation | convolution fusion | flops 4839702528 | bytes 14211072 | tf_op jit(solution)/shard_map/rcn,cnd->rd/dot_general | solution.py:24
  196.5 83.4 %all_to_all.9 = bf16[32,32,1536]{2,1,0:T(8,128)(2,1)S(1)} all-to-all(bf16[32,32,1536]{2,1,0:T(8,128)(2,1)S(1)} %bitcast.8), channel_id=1, replica_groups=mesh['dp'=8,'clus'=32] {'clus'}, dimensions={0} | all-to-all | bytes 6291456 | tf_op jit(solution)/shard_map/all_to_all | solution.py:27
  279.9 1.1 reduce_sum.12
  (2 shorter events, 0.0 us)
Async XLA Ops:
  6.5 81.4 %all-gather.2.cloned.1.call-start = ((), (), s32[]{:S(2)}) async-start(), calls=%async_computation.1 | async-start | bytes 3244032 | tf_op jit(solution)/shard_map/all_gather | solution.py:16
  7.3 180.6 %all-reduce.2.cloned.1.call-start = ((), (), s32[]{:S(2)}) async-start(), calls=%async_computation.2 | async-start | bytes 12582912 | tf_op jit(solution)/shard_map/psum | solution.py:20
  97.6 0.9 copy-start
  97.6 90.2 %copy-start.1 = (f32[12,128]{1,0:T(8,128)S(1)}, f32[12,128]{1,0:T(8,128)}, u32[]{:S(2)}) copy-start(f32[12,128]{1,0:T(8,128)} %param.8) | copy-start | bytes 18436
Sparse Core Ops, SparseCore 0:
  9.9 77.9 all-gather.1
  97.8 90.0 all-reduce.1
where the time goes:
time: 288 us
  waiting for transfers between devices  170 us (59%)
  blocking collectives  83.4 us (29%)
  matrix products  18.4 us (6%)
  between operations  13.4 us (5%)
    psum x1, waiting for transfers between devices, on_device(): summed = lax.psum(partial_pre, 'dp')  88.9 us
    all_to_all x1, blocking collectives, on_device(): lax.all_to_all(produced, 'clus', split_axis=0, concat_axis=0, tiled=True)  83.4 us
    all_gather x1, waiting for transfers between devices, on_device(): lax.all_gather(activations, 'clus', axis=0, tiled=True)  80.6 us
    dot_general x1, matrix products, on_device(): jnp.einsum('rd,cdn->rcn', lax.all_gather(activations, 'clus', axis=0, til...  9.73 us
    dot_general x1, matrix products, on_device(): jnp.einsum('rcn,cnd->rd', hidden, down_weight, preferred_element_type=jnp...  8.65 us
  transfers between devices with their start and end apart: 2, of which 2 were waited for; matrix products, arithmetic and copies ran while one was open for 0% of the time, Pallas kernels for 0%

commit v1 on v0

--- a/solution.py
+++ b/solution.py
@@ -1,7 +1,25 @@
+import functools
 import jax
 import jax.numpy as jnp
 from jax import lax
 from jax.sharding import PartitionSpec as P
+
+
+def feed_the_teams(xin, dimension_no):
+    oldest = lax.axis_size("clus")
+    local_part = lax.axis_index("clus")
+    vec_out, newest, everything = (oldest, local_part, xin.shape[dimension_no])
+    x_now, moved = (xin, 1)
+    while moved < vec_out:
+        current_block = lax.ppermute(
+            x_now, "clus", perm=[(at, (at - moved) % vec_out) for at in range(vec_out)]
+        )
+        x_now = jnp.concatenate([x_now, current_block], dimension_no)
+        moved = 2 * moved
+    return jnp.roll(x_now, newest * everything, dimension_no)
+
+
+shape_node = functools.partial(feed_the_teams, dimension_no=0)
 
 
 def on_device(activations, picks, up_weight, up_bias, down_weight):
@@ -12,10 +30,7 @@
     wanted = own_index * clusters_here + jnp.arange(clusters_here, dtype=jnp.int32)
     cluster_mask = jnp.any(picks[:, :, None] == wanted[None, None, :], axis=1).astype(jnp.float32)
     partial_pre = jnp.einsum(
-        "rd,cdn->rcn",
-        lax.all_gather(activations, "clus", axis=0, tiled=True),
-        up_weight,
-        preferred_element_type=jnp.float32,
+        "rd,cdn->rcn", shape_node(activations), up_weight, preferred_element_type=jnp.float32
     )
     summed = lax.psum(partial_pre, "dp")
     hidden = (jnp.maximum(summed + up_bias[None], 0.0) * cluster_mask[:, :, None]).astype(

time: 288 us -> 350 us (1.22)
  waiting for transfers between devices: 170 us -> 202 us
  starting transfers between devices: 0.04 us -> 16 us
  local copies, waits for them, and re-layouts: 0.89 us -> 12.4 us
    ppermute x0 -> x5, waiting for transfers between devices: none -> 97.4 us  [feed_the_teams(): lax.ppermute(x_now, 'clus', perm=[(at, (at - moved) % vec_out) for at in...]
    all_gather x1 -> x0, waiting for transfers between devices: 80.6 us -> none  [on_device(): lax.all_gather(activations, 'clus', axis=0, tiled=True)]
    psum x1, waiting for transfers between devices: 88.9 us -> 105 us  [on_device(): summed = lax.psum(partial_pre, 'dp')]
    ppermute x0 -> x5, starting transfers between devices: none -> 16 us  [feed_the_teams(): lax.ppermute(x_now, 'clus', perm=[(at, (at - moved) % vec_out) for at in...]
    unnamed x4 -> x16, local copies, waits for them, and re-layouts: 0.89 us -> 9.85 us
  transfers between devices with their start and end apart: 2 -> 6, of which waited for: 2 -> 6; matrix products, arithmetic and copies ran while one was open for 0% -> 1% of each run, Pallas kernels for 0% -> 0%
where the time goes in v1:
time: 350 us
  waiting for transfers between devices  202 us (58%)
  blocking collectives  83.4 us (24%)
  matrix products  18.3 us (5%)
  starting transfers between devices  16 us (5%)
  between operations  13.4 us (4%)
  local copies, waits for them, and re-layouts  12.4 us (4%)
  other arithmetic  4.27 us (1%)
    psum x1, waiting for transfers between devices, on_device(): summed = lax.psum(partial_pre, 'dp')  105 us
    ppermute x5, waiting for transfers between devices, feed_the_teams(): lax.ppermute(x_now, 'clus', perm=[(at, (at - moved) % vec_out) for at in...  97.4 us
    all_to_all x1, blocking collectives, on_device(): lax.all_to_all(produced, 'clus', split_axis=0, concat_axis=0, tiled=True)  83.4 us
    ppermute x5, starting transfers between devices, feed_the_teams(): lax.ppermute(x_now, 'clus', perm=[(at, (at - moved) % vec_out) for at in...  16 us
    unnamed x16, local copies, waits for them, and re-layouts  9.85 us
    dot_general x1, matrix products, on_device(): jnp.einsum('rd,cdn->rcn', shape_node(activations), up_weight, preferred_e...  9.69 us
    dot_general x1, matrix products, on_device(): jnp.einsum('rcn,cnd->rd', hidden, down_weight, preferred_element_type=jnp...  8.66 us
  transfers between devices with their start and end apart: 6, of which 6 were waited for; matrix products, arithmetic and copies ran while one was open for 1% of the time, Pallas kernels for 0%

profile of v1, /device:TPU:19, one launch (start us, length us, event | category | flops | bytes accessed | tf_op | source)
XLA Modules:
  0.0 350.2 jit_solution(11598879983751627764)
XLA Ops:
  6.5 0.2 collective-permute-start
  6.7 3.5 %collective-permute-done = bf16[32,1536]{1,0:T(8,128)(2,1)S(1)} collective-permute-done((bf16[32,1536]{1,0:T(8,128)(2,1)}, bf16[32,1536]{1,0:T(8,128)(2,1)S(1)}, u32[]{:S(2)}, u32[]{:S(2)}) %collective-permute-start) | collective-permute-done | bytes 98336 | tf_op jit(solution)/shard_map/ppermute | solution.py:14
  10.2 0.9 pad_maximum_fusion.2
  11.1 6.4 %collective-permute-start.1 = (bf16[64,1536]{1,0:T(8,128)(2,1)S(1)}, bf16[64,1536]{1,0:T(8,128)(2,1)S(1)}, u32[]{:S(2)}, u32[]{:S(2)}) collective-permute-start(bf16[64,1536]{1,0:T(8,128)(2,1)S(1)} %pad_maximum_fusion.2), channel_id=1, source_target_pairs={{0,30},{1,31},{2,0},{3,1},{4,2},{5,3},{6,4},{7,5},{8,6},{9,7},{10,... | collective-permute-start | bytes 589832 | tf_op jit(solution)/shard_map/ppermute | solution.py:14
  17.6 2.6 collective-permute-done.1
  20.2 0.9 pad_maximum_fusion.1
  21.1 4.8 %collective-permute-start.2 = (bf16[128,1536]{1,0:T(8,128)(2,1)S(1)}, bf16[128,1536]{1,0:T(8,128)(2,1)S(1)}, u32[]{:S(2)}, u32[]{:S(2)}) collective-permute-start(bf16[128,1536]{1,0:T(8,128)(2,1)S(1)} %pad_maximum_fusion.1), channel_id=1, source_target_pairs={{0,28},{1,29},{2,30},{3,31},{4,0},{5,1},{6,2},{7,3},{8,4},{9,5},{1... | collective-permute-start | bytes 1179656 | tf_op jit(solution)/shard_map/ppermute | solution.py:14
  25.9 5.4 %collective-permute-done.2 = bf16[128,1536]{1,0:T(8,128)(2,1)S(1)} collective-permute-done((bf16[128,1536]{1,0:T(8,128)(2,1)S(1)}, bf16[128,1536]{1,0:T(8,128)(2,1)S(1)}, u32[]{:S(2)}, u32[]{:S(2)}) %collective-permute-start.2) | collective-permute-done | bytes 393248 | tf_op jit(solution)/shard_map/ppermute | solution.py:14
  31.3 0.9 pad_maximum_fusion
  32.3 2.3 collective-permute-start.3
  34.6 1.6 constant_dynamic-update-slice_fusion.4
  36.2 0.7 constant_dynamic-update-slice_fusion.3
  36.8 0.8 constant_dynamic-update-slice_fusion.2
  37.6 1.0 constant_dynamic-update-slice_fusion.1
  38.6 16.2 %collective-permute-done.3 = bf16[256,1536]{1,0:T(8,128)(2,1)S(1)} collective-permute-done((bf16[256,1536]{1,0:T(8,128)(2,1)S(1)}, bf16[256,1536]{1,0:T(8,128)(2,1)S(1)}, u32[]{:S(2)}, u32[]{:S(2)}) %collective-permute-start.3) | collective-permute-done | bytes 786464 | tf_op jit(solution)/shard_map/ppermute | solution.py:14
  54.8 1.3 constant_dynamic-update-slice_fusion
  56.1 2.3 collective-permute-start.4
  58.4 69.6 %collective-permute-done.4 = bf16[512,1536]{1,0:T(8,128)(2,1)S(1)} collective-permute-done((bf16[512,1536]{1,0:T(8,128)(2,1)}, bf16[512,1536]{1,0:T(8,128)(2,1)S(1)}, u32[]{:S(2)}, u32[]{:S(2)}) %collective-permute-start.4) | collective-permute-done | bytes 1572896 | tf_op jit(solution)/shard_map/ppermute | solution.py:14
  128.0 1.3 constant_dynamic-update-slice_fusion.11
  129.3 0.6 constant_dynamic-update-slice_fusion.10
  129.9 0.6 constant_dynamic-update-slice_fusion.9
  130.6 0.7 constant_dynamic-update-slice_fusion.8
  131.3 0.8 constant_dynamic-update-slice_fusion.7
  132.0 0.9 constant_dynamic-update-slice_fusion.6
  133.0 1.3 constant_dynamic-update-slice_fusion.5
  134.2 9.7 %fusion = f32[1024,12,128]{2,0,1:T(8,128)} fusion(bf16[12,1536,128]{2,1,0:T(8,128)(2,1)} %param.7, bf16[2048,1536]{1,0:T(8,128)(2,1)} %constant_dynamic-update-slice_fusion.5, s32[]{:T(128)S(6)} %select_n.14), kind=kOutput, calls=%fused_computation.2 | convolution fusion | flops 4831838208 | bytes 14155780 | tf_op jit(solution)/shard_map/rd,cdn->rcn/dot_general | solution.py:32
  144.0 0.9 copy-done.1
  144.9 0.4 compare_reduce_fusion
  145.3 104.9 %all-reduce.2.cloned.1.call-done = f32[1024,12,128]{2,0,1:T(8,128)} async-done(((f32[1024,12,128]{2,0,1:T(8,128)}), f32[1024,12,128]{2,0,1:T(8,128)}) %all-reduce.2.cloned.1.call-update) | async-done | bytes 6291472 | tf_op jit(solution)/shard_map/psum | solution.py:35
  250.2 8.7 %bitcast_convert_fusion = bf16[1024,1536]{1,0:T(8,128)(2,1)S(1)} fusion(bf16[12,128,1536]{2,1,0:T(8,128)(2,1)} %param.9, f32[1024,12,128]{2,0,1:T(8,128)} %all-reduce.2.cloned.1.call-done, f32[1024,12]{0,1:T(8,128)S(1)} %convert_element_type.15, f32[12,128]{1,0:T(8,128)S(1)} %copy-done.2), kind=kOutput, calls=%fused_computation | convolution fusion | flops 4839702528 | bytes 14211072 | tf_op jit(solution)/shard_map/rcn,cnd->rd/dot_general | solution.py:39
  258.9 83.4 %all_to_all.9 = bf16[32,32,1536]{2,1,0:T(8,128)(2,1)S(1)} all-to-all(bf16[32,32,1536]{2,1,0:T(8,128)(2,1)S(1)} %bitcast.8), channel_id=1, replica_groups=mesh['dp'=8,'clus'=32] {'clus'}, dimensions={0} | all-to-all | bytes 6291456 | tf_op jit(solution)/shard_map/all_to_all | solution.py:42
  342.3 1.1 reduce_sum.12
  (9 shorter events, 0.0 us)
Async XLA Ops:
  6.5 122.8 %copy-start = (bf16[32,1536]{1,0:T(8,128)(2,1)S(1)}, bf16[32,1536]{1,0:T(8,128)(2,1)}, u32[]{:S(2)}) copy-start(bf16[32,1536]{1,0:T(8,128)(2,1)} %param.5) | copy-start | bytes 294916
  6.5 243.7 %all-reduce.2.cloned.1.call-start = ((), (), s32[]{:S(2)}) async-start(), calls=%async_computation.1 | async-start | bytes 12582912 | tf_op jit(solution)/shard_map/psum | solution.py:35
  6.5 3.7 %collective-permute-start = (bf16[32,1536]{1,0:T(8,128)(2,1)}, bf16[32,1536]{1,0:T(8,128)(2,1)S(1)}, u32[]{:S(2)}, u32[]{:S(2)}) collective-permute-start(bf16[32,1536]{1,0:T(8,128)(2,1)} %param.5), channel_id=1, source_target_pairs={{0,31},{1,0},{2,1},{3,2},{4,3},{5,4},{6,5},{7,6},{8,7},{9,8},{10,9... | collective-permute-start | bytes 294920 | tf_op jit(solution)/shard_map/ppermute | solution.py:14
  11.1 9.1 %collective-permute-start.1 = (bf16[64,1536]{1,0:T(8,128)(2,1)S(1)}, bf16[64,1536]{1,0:T(8,128)(2,1)S(1)}, u32[]{:S(2)}, u32[]{:S(2)}) collective-permute-start(bf16[64,1536]{1,0:T(8,128)(2,1)S(1)} %pad_maximum_fusion.2), channel_id=1, source_target_pairs={{0,30},{1,31},{2,0},{3,1},{4,2},{5,3},{6,4},{7,5},{8,6},{9,7},{10,... | collective-permute-start | bytes 589832 | tf_op jit(solution)/shard_map/ppermute | solution.py:14
  21.1 10.2 %collective-permute-start.2 = (bf16[128,1536]{1,0:T(8,128)(2,1)S(1)}, bf16[128,1536]{1,0:T(8,128)(2,1)S(1)}, u32[]{:S(2)}, u32[]{:S(2)}) collective-permute-start(bf16[128,1536]{1,0:T(8,128)(2,1)S(1)} %pad_maximum_fusion.1), channel_id=1, source_target_pairs={{0,28},{1,29},{2,30},{3,31},{4,0},{5,1},{6,2},{7,3},{8,4},{9,5},{1... | collective-permute-start | bytes 1179656 | tf_op jit(solution)/shard_map/ppermute | solution.py:14
  32.3 22.5 %collective-permute-start.3 = (bf16[256,1536]{1,0:T(8,128)(2,1)S(1)}, bf16[256,1536]{1,0:T(8,128)(2,1)S(1)}, u32[]{:S(2)}, u32[]{:S(2)}) collective-permute-start(bf16[256,1536]{1,0:T(8,128)(2,1)S(1)} %pad_maximum_fusion), channel_id=1, source_target_pairs={{0,24},{1,25},{2,26},{3,27},{4,28},{5,29},{6,30},{7,31},{8,0},{9,1... | collective-permute-start | bytes 2359304 | tf_op jit(solution)/shard_map/ppermute | solution.py:14
  56.1 71.9 %collective-permute-start.4 = (bf16[512,1536]{1,0:T(8,128)(2,1)}, bf16[512,1536]{1,0:T(8,128)(2,1)S(1)}, u32[]{:S(2)}, u32[]{:S(2)}) collective-permute-start(bf16[512,1536]{1,0:T(8,128)(2,1)} %get-tuple-element.5), channel_id=1, source_target_pairs={{0,16},{1,17},{2,18},{3,19},{4,20},{5,21},{6,22},{7,23},{8,24},{9,... | collective-permute-start | bytes 4718600 | tf_op jit(solution)/shard_map/ppermute | solution.py:14
  143.9 0.9 copy-start.1
  143.9 106.3 %copy-start.2 = (f32[12,128]{1,0:T(8,128)S(1)}, f32[12,128]{1,0:T(8,128)}, u32[]{:S(2)}) copy-start(f32[12,128]{1,0:T(8,128)} %param.8) | copy-start | bytes 18436
Sparse Core Ops, SparseCore 0:
  144.1 106.0 all-reduce.1

commit v2 on v0

--- a/solution.py
+++ b/solution.py
@@ -17,7 +17,10 @@
         up_weight,
         preferred_element_type=jnp.float32,
     )
-    summed = lax.psum(partial_pre, "dp")
+    size, summed = (lax.axis_size("dp"), partial_pre)
+    for far in [1 << k for k in range(size.bit_length() - 1)]:
+        swap = [(i, i ^ far) for i in range(size)]
+        summed = summed + lax.ppermute(summed, "dp", swap)
     hidden = (jnp.maximum(summed + up_bias[None], 0.0) * cluster_mask[:, :, None]).astype(
         jnp.bfloat16
     )

time: 288 us -> 485 us (1.68)
  waiting for transfers between devices: 170 us -> 363 us
  blocking collectives: 83.4 us -> 76.8 us
  starting transfers between devices: 0.04 us -> 6.16 us
    ppermute x0 -> x3, waiting for transfers between devices: none -> 282 us  [on_device(): summed = summed + lax.ppermute(summed, 'dp', swap)]
    psum x1 -> x0, waiting for transfers between devices: 88.9 us -> none  [on_device(): summed = lax.psum(partial_pre, 'dp')]
    all_to_all x1, blocking collectives: 83.4 us -> 76.8 us  [on_device(): lax.all_to_all(produced, 'clus', split_axis=0, concat_axis=0, tiled=True)]
    ppermute x0 -> x3, starting transfers between devices: none -> 6.15 us  [on_device(): summed = summed + lax.ppermute(summed, 'dp', swap)]
  transfers between devices with their start and end apart: 2 -> 4, of which waited for: 2 -> 4; matrix products, arithmetic and copies ran while one was open for 0% -> 0% of each run, Pallas kernels for 0% -> 0%
where the time goes in v2:
time: 485 us; the launch traced here: 482 us
  waiting for transfers between devices  363 us (75%)
  blocking collectives  76.8 us (16%)
  matrix products  17.4 us (4%)
  between operations  13.4 us (3%)
  starting transfers between devices  6.16 us (1%)
  other arithmetic  5.42 us (1%)
    ppermute x3, waiting for transfers between devices, on_device(): summed = summed + lax.ppermute(summed, 'dp', swap)  282 us
    all_gather x1, waiting for transfers between devices, on_device(): lax.all_gather(activations, 'clus', axis=0, tiled=True)  80.6 us
    all_to_all x1, blocking collectives, on_device(): lax.all_to_all(produced, 'clus', split_axis=0, concat_axis=0, tiled=True)  76.8 us
  transfers between devices with their start and end apart: 4, of which 4 were waited for; matrix products, arithmetic and copies ran while one was open for 0% of the time, Pallas kernels for 0%

profile of v2, /device:TPU:19, one launch (start us, length us, event | category | flops | bytes accessed | tf_op | source)
XLA Modules:
  0.0 482.2 jit_solution(11523214223139447040)
XLA Ops:
  6.5 0.0 all-gather.2.cloned.1.call-start
  6.5 0.7 all-gather.2.cloned.1.call-update
  7.3 80.6 %all-gather.2.cloned.1.call-done = bf16[1024,1536]{1,0:T(8,128)(2,1)} async-done(((bf16[32,1536]{1,0:T(8,128)(2,1)}), bf16[1024,1536]{1,0:T(8,128)(2,1)}) %all-gather.2.cloned.1.call-update) | async-done | bytes 3145744 | tf_op jit(solution)/shard_map/all_gather | solution.py:16
  87.9 7.8 %fusion = f32[1024,12,128]{2,0,1:T(8,128)S(1)} fusion(bf16[12,1536,128]{2,1,0:T(8,128)(2,1)} %param.7, bf16[1024,1536]{1,0:T(8,128)(2,1)} %all-gather.2.cloned.1.call-done), kind=kOutput, calls=%fused_computation.2 | convolution fusion | flops 4831838208 | bytes 14155776 | tf_op jit(solution)/shard_map/rd,cdn->rcn/dot_general | solution.py:14
  95.7 4.0 collective-permute-start
  99.7 9.8 %collective-permute-done = f32[1024,12,128]{2,0,1:T(8,128)S(1)} collective-permute-done((f32[1024,12,128]{2,0,1:T(8,128)S(1)}, f32[1024,12,128]{2,0,1:T(8,128)S(1)}, u32[]{:S(2)}, u32[]{:S(2)}) %collective-permute-start) | collective-permute-done | bytes 6291488 | tf_op jit(solution)/shard_map/ppermute | solution.py:23
  109.5 0.6 add.27
  110.2 0.0 copy-start
  110.2 0.0 copy-start.1
  110.2 0.4 collective-permute-start.1
  110.5 136.5 %collective-permute-done.1 = f32[1024,12,128]{2,0,1:T(8,128)S(1)} collective-permute-done((f32[1024,12,128]{2,0,1:T(8,128)S(1)}, f32[1024,12,128]{2,0,1:T(8,128)S(1)}, u32[]{:S(2)}, u32[]{:S(2)}) %collective-permute-start.1) | collective-permute-done | bytes 6291488 | tf_op jit(solution)/shard_map/ppermute | solution.py:23
  247.0 3.3 add.28
  250.3 1.8 collective-permute-start.2
  252.1 0.0 copy-done
  252.1 0.4 compare_reduce_fusion
  252.5 135.4 %collective-permute-done.2 = f32[1024,12,128]{2,0,1:T(8,128)} collective-permute-done((f32[1024,12,128]{2,0,1:T(8,128)}, f32[1024,12,128]{2,0,1:T(8,128)}, u32[]{:S(2)}, u32[]{:S(2)}) %collective-permute-start.2) | collective-permute-done | bytes 6291488 | tf_op jit(solution)/shard_map/ppermute | solution.py:23
  387.9 0.0 copy-done.1
  387.9 9.6 %bitcast_convert_fusion = bf16[1024,1536]{1,0:T(8,128)(2,1)S(1)} fusion(bf16[12,128,1536]{2,1,0:T(8,128)(2,1)} %param.9, f32[1024,12,128]{2,0,1:T(8,128)} %add.28, f32[1024,12,128]{2,0,1:T(8,128)} %collective-permute-done.2, f32[1024,12]{0,1:T(8,128)S(1)} %convert_element_type.15, f32[12,128]{1,0:T(8,128)S(1)} %copy-done.1), kind=kOutput, calls=%fused_computation | convolution fusion | flops 4841275392 | bytes 20502528 | tf_op jit(solution)/shard_map/rcn,cnd->rd/dot_general | solution.py:27
  397.5 76.8 %all_to_all.9 = bf16[32,32,1536]{2,1,0:T(8,128)(2,1)S(1)} all-to-all(bf16[32,32,1536]{2,1,0:T(8,128)(2,1)S(1)} %bitcast.8), channel_id=1, replica_groups=mesh['dp'=8,'clus'=32] {'clus'}, dimensions={0} | all-to-all | bytes 6291456 | tf_op jit(solution)/shard_map/all_to_all | solution.py:30
  474.3 1.1 reduce_sum.12
  (2 shorter events, 0.0 us)
Async XLA Ops:
  6.5 81.4 %all-gather.2.cloned.1.call-start = ((), (), s32[]{:S(2)}) async-start(), calls=%async_computation.1 | async-start | bytes 3244032 | tf_op jit(solution)/shard_map/all_gather | solution.py:16
  95.7 13.8 %collective-permute-start = (f32[1024,12,128]{2,0,1:T(8,128)S(1)}, f32[1024,12,128]{2,0,1:T(8,128)S(1)}, u32[]{:S(2)}, u32[]{:S(2)}) collective-permute-start(f32[1024,12,128]{2,0,1:T(8,128)S(1)} %fusion), channel_id=1, source_target_pairs={{0,32},{32,0},{64,96},{96,64},{128,160},{160,128},{192,224},{224,1... | collective-permute-start | bytes 18874376 | tf_op jit(solution)/shard_map/ppermute | solution.py:23
  110.2 141.9 %copy-start = (s32[1024,48]{0,1:T(8,128)S(1)}, s32[1024,48]{0,1:T(8,128)}, u32[]{:S(2)}) copy-start(s32[1024,48]{0,1:T(8,128)} %param.6) | copy-start | bytes 589828
  110.2 277.7 %copy-start.1 = (f32[12,128]{1,0:T(8,128)S(1)}, f32[12,128]{1,0:T(8,128)}, u32[]{:S(2)}) copy-start(f32[12,128]{1,0:T(8,128)} %param.8) | copy-start | bytes 18436
  110.2 136.8 %collective-permute-start.1 = (f32[1024,12,128]{2,0,1:T(8,128)S(1)}, f32[1024,12,128]{2,0,1:T(8,128)S(1)}, u32[]{:S(2)}, u32[]{:S(2)}) collective-permute-start(f32[1024,12,128]{2,0,1:T(8,128)S(1)} %add.27), channel_id=1, source_target_pairs={{0,64},{32,96},{64,0},{96,32},{128,192},{160,224},{192,128},{224,1... | collective-permute-start | bytes 18874376 | tf_op jit(solution)/shard_map/ppermute | solution.py:23
  250.3 137.6 %collective-permute-start.2 = (f32[1024,12,128]{2,0,1:T(8,128)}, f32[1024,12,128]{2,0,1:T(8,128)}, u32[]{:S(2)}, u32[]{:S(2)}) collective-permute-start(f32[1024,12,128]{2,0,1:T(8,128)} %add.28), channel_id=1, source_target_pairs={{0,128},{32,160},{64,192},{96,224},{128,0},{160,32},{192,64},{224,... | collective-permute-start | bytes 18874376 | tf_op jit(solution)/shard_map/ppermute | solution.py:23
Sparse Core Ops, SparseCore 0:
  9.9 77.9 all-gather.1
